TPU v7x, 32 devices: a whole 2x2x4 slice. The times are simulated.
32 devices in a mesh: expert: 8 (over y, x, core), hidden: 4 (over z).
Axes of the slice: x: 2, y: 2, z: 4, core: 2. Of those that a mesh axis runs over, the one named last changes fastest.
Arguments:
- tokens: bfloat16 [8192, 1024], P(('expert', 'hidden')), may hold values from -6 to 6
- assignment: int32 [8192, 1], P(('expert', 'hidden')), may hold values from 0 to 15; in each aligned block of 256 rows (0 to 255, 256 to 511, ...) at most 18 rows name the same one
- lengths: int32 [8], replicated, may hold values from 32 to 1024
- centroids: bfloat16 [16, 1024], P('expert', 'hidden'), may hold values from -0.125 to 0.125
- ln_gain: float32 [16, 1024], P('expert', 'hidden'), may hold values from 0.5 to 1.5
- ln_bias: float32 [16, 1024], P('expert', 'hidden'), may hold values from -2 to 2
- w_in: bfloat16 [16, 1024, 4096], P('expert', None, 'hidden'), may hold values from -0.1875 to 0.1875
- b_in: float32 [16, 4096], P('expert', 'hidden'), may hold values from -2 to 2
- w_out: bfloat16 [16, 4096, 1024], P('expert', 'hidden'), may hold values from -0.1875 to 0.1875
- b_out: float32 [16, 1024], P('expert', 'hidden'), may hold values from -2 to 2
- cotangent: bfloat16 [8192, 1024], P(('expert', 'hidden')), may hold values from -6 to 6
Outputs:
- mixed: bfloat16 [8192, 1024], P(('expert', 'hidden'))
- tokens_grad: bfloat16 [8192, 1024], P(('expert', 'hidden'))
- centroids_grad: float32 [16, 1024], P('expert', 'hidden')
- ln_gain_grad: float32 [16, 1024], P('expert', 'hidden')
- ln_bias_grad: float32 [16, 1024], P('expert', 'hidden')
- w_in_grad: float32 [16, 1024, 4096], P('expert', None, 'hidden')
- b_in_grad: float32 [16, 4096], P('expert', 'hidden')
- w_out_grad: float32 [16, 4096, 1024], P('expert', 'hidden')
- b_out_grad: float32 [16, 1024], P('expert', 'hidden')
- mean_gate: float32 [16], replicated
Inputs may be any that keep to these rules, and one draw needn't show every extreme that they name: `assignment`: in each aligned block of 256 rows (the rows of one device) no expert is named by more than 18 rows, a bound that some block reaches; every expert is named by some row.
All inputs are finite; a program needn't handle non-finite values.
Results may differ from a plain program's by a relative error of at most 0.0061.
Values may be sent and summed in bfloat16 or wider, within the bound.
A program may use at most 128 MiB of HBM per device.

v0:
```python
import functools

import jax
import jax.numpy as jnp
from jax import lax
from jax.experimental import pallas as pl
from jax.experimental.pallas import tpu as pltpu
from jax.sharding import PartitionSpec as P

EPS = 1e-05
MESH = pl.DeviceIdType.MESH
F32 = jnp.float32
BF16 = jnp.bfloat16
TILE = 256
PIECES = 3
GELU_A = 0.7978845608028654
GELU_B = 0.044715
SHAPES = ((8, 8, 8, 8), (8, 7, 6, 5), (8, 6, 4, 3),)


def contract(a, b, dims=((1,), (0,))):
    return lax.dot_general(a, b, (dims, ((), ())), preferred_element_type=F32)


def iota(shape, axis):
    return lax.broadcasted_iota(jnp.int32, shape, axis)


def ones_where(mask):
    return mask.astype(F32).astype(BF16)


def per(index, size, count):
    return jnp.floor((index.astype(F32) + 0.5) * (1.0 / size)).astype(jnp.int32)


def layer_kernel(
    dims, sizes,
    asg, lens, cent, gain, bias, bout, bin_, tok_in, cot_in, win, wout,
    home, ret, o_slot, o_cent, o_gain, o_bias, o_win, o_bin, o_wout, o_bout, o_mean,
    vwin, vwout, gat, act, pg, sbuf, rbuf, snd, rcv, xg, spread, pick, unpick, pick_count,
    par, stats, zs, mg, grads, gbuf, normed_of, turned,
    w_sem, par_s, par_r, zs_s, zs_r, mg_s, mg_r, gb_s, gb_r,
    disp_s, disp_r, ret_s, ret_r, gat_s, gat_r, red_s, red_r,
):
    G, H, J, S, MSG, R, T, D, F, PW, seq_len = dims
    e, z = lax.axis_index("expert"), lax.axis_index("hidden")
    E, GM, N = G * J, G * MSG, H * R
    parts = D // TILE
    BLOCK = R

    def cols(t, size=TILE):
        return pl.ds(pl.multiple_of(t * size, size), size)

    def rows(start, size):
        return pl.ds(pl.multiple_of(start, 16), size)

    def loop(count, body):
        def step(i, _):
            body(i)
            return 0

        lax.fori_loop(0, count, step, 0)

    barrier = pltpu.get_barrier_semaphore()
    for d in range(1, H):
        pl.semaphore_signal(barrier, inc=1, device_id=(e, (z + d) % H), device_id_type=MESH)
    for d in range(1, G):
        pl.semaphore_signal(barrier, inc=1, device_id=((e + d) % G, z), device_id_type=MESH)

    loads = []
    for a, source in enumerate((tok_in, cot_in)):
        for part in range(parts):
            loads.append(pltpu.make_async_copy(
                source.at[:, pl.ds(part * TILE, TILE)], home.at[a, pl.ds(part * T, T), :],
                w_sem.at[a * parts + part]))
    weights = [
        pltpu.make_async_copy(win, vwin, w_sem.at[2 * parts]),
        pltpu.make_async_copy(wout, vwout, w_sem.at[2 * parts + 1]),
    ]
    for copy in loads + weights:
        copy.start()

    own_cols = cols(z, PW)
    par[pl.ds(0, J), own_cols] = gain[...]
    par[pl.ds(J, J), own_cols] = bias[...]
    par[pl.ds(2 * J, J), own_cols] = cent[...].astype(F32)
    par[pl.ds(3 * J, J), own_cols] = bout[...]

    expert = asg[...]
    place = (e * H + z) * T
    length = lens[place // seq_len]
    live = (place % seq_len + iota((1, T), 1)) < length
    sub_e = iota((E, 1), 0)
    hot = ((expert == sub_e) & live).astype(F32)
    earlier = ones_where(iota((T, T), 0) < iota((T, T), 1))
    before = contract(hot.astype(BF16), earlier)
    group = per(sub_e, J, G)
    inner = sub_e - group * J
    rank = jnp.sum(hot * before, axis=0, keepdims=True).astype(jnp.int32)
    to_group = jnp.sum(hot * group.astype(F32), axis=0, keepdims=True).astype(jnp.int32)
    to_inner = jnp.sum(hot * inner.astype(F32), axis=0, keepdims=True).astype(jnp.int32)
    to_inner = jnp.where(live, to_inner, -1)
    message = to_group * MSG
    o_slot[...] = jnp.broadcast_to(jnp.where(live, to_inner * GM + message + rank, -D * D), (8, T))

    pl.semaphore_wait(barrier, (H - 1) + (G - 1))

    def par_copy(d, source):
        return pltpu.make_async_remote_copy(
            src_ref=par.at[:, cols(source, PW)], dst_ref=par.at[:, cols(source, PW)],
            send_sem=par_s.at[d], recv_sem=par_r.at[d],
            device_id=(e, (z + d) % H), device_id_type=MESH)

    for d in range(1, H):
        par_copy(d, z).start()

    def msg(k):
        return pl.ds(pl.multiple_of(k * MSG, MSG), MSG)

    def disp_copy(j, a, d, target):
        return pltpu.make_async_remote_copy(
            src_ref=snd.at[j, a, msg(target)], dst_ref=rcv.at[j, a, msg(e)],
            send_sem=disp_s.at[j, a, d], recv_sem=disp_r.at[j, a, d],
            device_id=(target, z), device_id_type=MESH)

    def disp_in(j, a, d):
        k = (e - d + G) % G
        return pltpu.make_async_remote_copy(
            src_ref=snd.at[j, a, msg(k)], dst_ref=rcv.at[j, a, msg(k)],
            send_sem=disp_s.at[j, a, d], recv_sem=disp_r.at[j, a, d],
            device_id=((e + d) % G, z), device_id_type=MESH)

    def dispatch(i):
        j, a = i // 2, i % 2
        row = iota((GM, T), 0)
        mine = to_inner == j

        @pl.when(a == 0)
        def _():
            at = jnp.where(mine, message + rank, -D * D)
            for part in range(parts):
                spread[:, pl.ds(part * T, T)] = ones_where(at + part * S == row)

        for b in range(2):
            @pl.when(jnp.logical_and(j == 0, a == b))
            def _(b=b):
                for copy in loads[b * parts:(b + 1) * parts]:
                    copy.wait()

        counted = jnp.where(mine & (a == 0), message + parts * S, -1)
        v = contract(spread[...], home[a]) + contract(ones_where(counted == row), jnp.ones((T, TILE), BF16))
        snd[j, a] = v.astype(BF16)
        for d in range(1, G):
            disp_copy(j, a, d, (e + d) % G).start()
        rcv[j, a, msg(e), :] = snd[j, a, msg(e), :]

    loop(2 * J, dispatch)

    def row_of(c):
        k = per(c, MSG, G)
        start = jnp.full(c.shape, -D * D, jnp.int32)
        filled_before = jnp.int32(0)
        for i in range(G):
            first = (i * H + z) * T
            some = lens[first // seq_len] > first % seq_len
            start = jnp.where((k == i) & some, filled_before * S, start)
            filled_before = filled_before + some.astype(jnp.int32)
        return start, c - k * MSG

    start, within = row_of(iota((1, GM), 1))
    down = iota((R, GM), 0)
    for part in range(parts):
        i = within - part * S
        pick[pl.ds(part * R, R), :] = ones_where(jnp.where((i >= 0) & (i < S), start + i, -1) == down)
    counts_at = jnp.where(within == parts * S, start, -D * D)
    pick_count[...] = ones_where((down >= counts_at) & (down < counts_at + S))
    start, within = row_of(iota((GM, 1), 0))
    across = iota((1, parts * R), 1)
    across_part = per(across, R, parts)
    i = within - across_part * S
    unpick[...] = ones_where((i >= 0) & (i < S) & (start + i == across - across_part * R))

    for h in range(H):
        if sizes[h] < R:
            gat[:, :, pl.ds(h * R + sizes[h], R - sizes[h]), :] = jnp.zeros((2, J, R - sizes[h], D), BF16)

    def clear(slot_at):
        def one(i):
            rbuf[i // J, i % J, slot_at] = jnp.zeros((R, D), BF16)

        loop(2 * J, one)

    pl.when(z == 0)(lambda: clear(H))
    pl.when(z == H - 1)(lambda: clear(H - 1))

    o_bin[...] = jnp.zeros_like(o_bin)

    for d in range(1, H):
        par_copy(d, (z - d + H) % H).wait_recv()

    def with_rows(chunk, body):
        for size in sorted(set(sizes)):
            planes = [h for h in range(H) if sizes[h] == size]
            if len(planes) == H:
                body(size)
            else:
                hit = chunk == planes[0]
                for h in planes[1:]:
                    hit = jnp.logical_or(hit, chunk == h)
                pl.when(hit)(functools.partial(body, size))

    def gat_copy(a, j, chunk, up, size):
        at = (a, j, rows(chunk * R, size))
        return pltpu.make_async_remote_copy(
            src_ref=gat.at[at], dst_ref=gat.at[at],
            send_sem=gat_s.at[up, a, j, chunk], recv_sem=gat_r.at[a, j, chunk],
            device_id=(e, jnp.clip(z + 2 * up - 1, 0, H - 1)), device_id_type=MESH)

    def send_gat(a, j, chunk, up, size):
        @pl.when(jnp.where(up == 1, z < H - 1, z > 0))
        def _():
            gat_copy(a, j, chunk, up, size).start()

    def send_own(a, j):
        def both(size):
            send_gat(a, j, z, 1, size)
            send_gat(a, j, z, 0, size)

        with_rows(z, both)

    def piece_of(size, piece):
        start = 0
        for i in range(piece + 1):
            count = -(-(size - start) // (16 * (PIECES - i))) * 16
            start = start + count
        return start - count, count

    def red_copy(a, j, piece, to, up, size):
        slot_to = jnp.where(jnp.logical_and(up == 1, to == z + 1), H, to)
        at = pl.ds(*piece_of(size, piece))
        return pltpu.make_async_remote_copy(
            src_ref=sbuf.at[a, j, to, at], dst_ref=rbuf.at[a, j, slot_to, at],
            send_sem=red_s.at[a, j, piece, to], recv_sem=red_r.at[a, j, piece, slot_to],
            device_id=(e, jnp.clip(z + 2 * up - 1, 0, H - 1)), device_id_type=MESH)

    def red_in(a, j, piece, slot_at, size):
        at = pl.ds(*piece_of(size, piece))
        return pltpu.make_async_remote_copy(
            src_ref=sbuf.at[a, j, 0, at], dst_ref=rbuf.at[a, j, slot_at, at],
            send_sem=red_s.at[a, j, piece, 0], recv_sem=red_r.at[a, j, piece, slot_at],
            device_id=(e, jnp.clip(z + 1, 0, H - 1)), device_id_type=MESH)

    def quarter(part, b):
        return pl.ds(pl.multiple_of(part * R + b * BLOCK, 16), BLOCK)

    lane8 = iota((8, 128), 1)
    r1 = iota((R, 1), 0)
    rank_in = (r1 - S * per(r1, S, G)).astype(F32)
    zs[z] = jnp.zeros((16, 128), F32)

    def take_in(j, a):
        for d in range(1, G):
            disp_in(j, a, d).wait_recv()
        xg[j, a] = contract(pick[...], rcv[j, a]).astype(BF16)

    def prepare(j):
        take_in(j, 0)
        count = contract(pick_count[...], rcv[j, 0, :, pl.ds(0, 128)])[:, 0:1]
        stats[3, j] = (rank_in < count).astype(F32)

        def block(b):
            x = [xg[j, 0, quarter(part, b), :].astype(F32) for part in range(parts)]
            mean = sum(jnp.sum(v, axis=1, keepdims=True) for v in x) * (1.0 / D)
            x_mid = [v - mean for v in x]
            var = sum(jnp.sum(v * v, axis=1, keepdims=True) for v in x_mid) * (1.0 / D)
            factor = lax.rsqrt(var + EPS)
            score = 0.0
            at = rows(b * BLOCK, BLOCK)
            for part in range(parts):
                lanes = pl.ds(part * TILE, TILE)
                normed = x_mid[part] * factor
                lifted = normed * par[pl.ds(j, 1), lanes] + par[pl.ds(J + j, 1), lanes]
                gat[0, j, rows(z * R + b * BLOCK, BLOCK), lanes] = lifted.astype(BF16)
                normed_of[j, at, lanes] = normed
                score = score + jnp.sum(x[part] * par[pl.ds(2 * J + j, 1), lanes], axis=1, keepdims=True)
            stats[0, j, at] = jax.nn.sigmoid(score)
            stats[1, j, at] = factor

        loop(R // BLOCK, block)
        send_own(0, j)
        take_in(j, 1)

        def weigh(b):
            at = rows(b * BLOCK, BLOCK)
            for part in range(parts):
                g = xg[j, 1, quarter(part, b), :].astype(F32)
                gat[1, j, rows(z * R + b * BLOCK, BLOCK), pl.ds(part * TILE, TILE)] = (stats[0, j, at] * g).astype(BF16)

        loop(R // BLOCK, weigh)
        send_own(1, j)
        total = jnp.sum(stats[3, j] * stats[0, j], axis=0, keepdims=True)
        number = jnp.sum(stats[3, j], axis=0, keepdims=True)
        zs[z, pl.ds(0, 8), :] += jnp.where(lane8 == j, total, 0.0)
        zs[z, pl.ds(8, 8), :] += jnp.where(lane8 == j, number, 0.0)

    loop(J, prepare)

    def zs_copy(d, source):
        return pltpu.make_async_remote_copy(
            src_ref=zs.at[source], dst_ref=zs.at[source],
            send_sem=zs_s.at[d], recv_sem=zs_r.at[d],
            device_id=(e, (z + d) % H), device_id_type=MESH)

    for d in range(1, H):
        zs_copy(d, z).start()

    for copy in weights:
        copy.wait()

    wide = 2 * TILE

    def compute(chunk, j):
        mine = rows(chunk * R, R)

        def first(t):
            pre = contract(gat[0, j, mine, :], vwin[j, :, cols(t, wide)]) + bin_[pl.ds(j, 1), cols(t, wide)]
            sq = pre * pre
            th = jnp.tanh(pre * (GELU_A + (GELU_A * GELU_B) * sq))
            cdf = 0.5 + 0.5 * th
            slope = cdf + pre * (0.5 - 0.5 * th * th) * (GELU_A + (3.0 * GELU_A * GELU_B) * sq)
            act[j, mine, cols(t, wide)] = (pre * cdf).astype(BF16)
            act_grad = contract(gat[1, j, mine, :], vwout[j, cols(t, wide), :], ((1,), (1,)))
            pre_grad = (act_grad * slope).astype(BF16)
            pg[j, mine, cols(t, wide)] = pre_grad
            o_bin[pl.ds(j, 1), cols(t, wide)] += jnp.sum(pre_grad.astype(F32), axis=0, keepdims=True)

        loop(F // wide, first)

        def second(t):
            v = contract(act[j, mine, :], vwout[j, :, cols(t, wide)])
            sbuf[0, j, chunk, :, cols(t, wide)] = v.astype(BF16)
            w = contract(pg[j, mine, :], vwin[j, cols(t, wide), :], ((1,), (1,)))
            sbuf[1, j, chunk, :, cols(t, wide)] = w.astype(BF16)

        loop(D // wide, second)

    def outer(left, right, to, tall, wide):
        turned[pl.ds(0, tall), :] = jnp.transpose(left)

        def tile(t):
            to[:, cols(t)] = contract(turned[pl.ds(0, tall), :], right[:, cols(t)])

        loop(wide // TILE, tile)

    def mg_copy(d, source):
        return pltpu.make_async_remote_copy(
            src_ref=mg.at[source], dst_ref=mg.at[source],
            send_sem=mg_s.at[d], recv_sem=mg_r.at[d],
            device_id=((e + d) % G, z), device_id_type=MESH)

    def gb_copy(d, source, target):
        return pltpu.make_async_remote_copy(
            src_ref=grads.at[:, cols(target, PW)], dst_ref=gbuf.at[source],
            send_sem=gb_s.at[d], recv_sem=gb_r.at[d],
            device_id=(e, (z + d) % H), device_id_type=MESH)

    def ret_copy(j, a, d, target):
        return pltpu.make_async_remote_copy(
            src_ref=snd.at[j, a, msg(target)], dst_ref=ret.at[a, rows(j * GM + e * MSG, MSG)],
            send_sem=ret_s.at[j, a, d], recv_sem=ret_r.at[j, a, d],
            device_id=(target, z), device_id_type=MESH)

    def ret_in(j, a, d):
        k = (e - d + G) % G
        return pltpu.make_async_remote_copy(
            src_ref=snd.at[j, a, msg(k)], dst_ref=ret.at[a, rows(j * GM + k * MSG, MSG)],
            send_sem=ret_s.at[j, a, d], recv_sem=ret_r.at[j, a, d],
            device_id=((e + d) % G, z), device_id_type=MESH)

    def wait_sums(a, j):
        def both(size):
            for piece in range(PIECES):
                @pl.when(z < H - 1)
                def _(piece=piece):
                    red_in(a, j, piece, z, size).wait_recv()

                @pl.when(z > 0)
                def _(piece=piece):
                    red_in(a, j, piece, H, size).wait_recv()

        with_rows(z, both)

    def summed(a, j, b, part):
        at = (rows(b * BLOCK, BLOCK), pl.ds(part * TILE, TILE))
        v = sbuf[(a, j, z, *at)].astype(F32) + rbuf[(a, j, z, *at)].astype(F32) + rbuf[(a, j, H, *at)].astype(F32)
        return jnp.where(stats[3, j, at[0]] > 0.5, v, 0.0)

    def send_home(j, a):
        snd[j, a] = contract(unpick[...], xg[j, a]).astype(BF16)
        for d in range(1, G):
            ret_copy(j, a, d, (e + d) % G).start()
        ret[a, rows(j * GM + e * MSG, MSG), :] = snd[j, a, msg(e), :]

    def finish(j):
        wait_sums(0, j)

        def forward(b):
            at = rows(b * BLOCK, BLOCK)
            gate = stats[0, j, at]
            gate_grad = 0.0
            for part in range(parts):
                lanes = pl.ds(part * TILE, TILE)
                branch = (summed(0, j, b, part) + par[pl.ds(3 * J + j, 1), lanes]).astype(BF16).astype(F32)
                x = xg[j, 0, quarter(part, b), :].astype(F32)
                gate_grad = gate_grad + jnp.sum(
                    xg[j, 1, quarter(part, b), :].astype(F32) * branch, axis=1, keepdims=True)
                rbuf[0, j, H, at, lanes] = x.astype(BF16)
                xg[j, 0, quarter(part, b), :] = (x + gate * branch).astype(BF16)
            score_grad = gate_grad * gate * (1.0 - gate)
            stats[2, j, at] = score_grad
            for part in range(parts):
                lanes = pl.ds(part * TILE, TILE)
                x = rbuf[0, j, H, at, lanes].astype(F32)
                grads[pl.ds(2 * J + j, 1), lanes] += jnp.sum(score_grad * x, axis=0, keepdims=True)
                sent = gat[1, j, rows(z * R + b * BLOCK, BLOCK), lanes].astype(F32)
                grads[pl.ds(3 * J + j, 1), lanes] += jnp.sum(sent, axis=0, keepdims=True)

        loop(R // BLOCK, forward)
        send_home(j, 0)
        wait_sums(1, j)

        def backward(b):
            at = rows(b * BLOCK, BLOCK)
            factor, score_grad = stats[1, j, at], stats[2, j, at]
            sum_n, sum_nn = 0.0, 0.0
            n_grads = []
            for part in range(parts):
                lanes = pl.ds(part * TILE, TILE)
                lifted_grad = summed(1, j, b, part)
                normed = normed_of[j, at, lanes]
                grads[pl.ds(j, 1), lanes] += jnp.sum(lifted_grad * normed, axis=0, keepdims=True)
                grads[pl.ds(J + j, 1), lanes] += jnp.sum(lifted_grad, axis=0, keepdims=True)
                n_grad = lifted_grad * par[pl.ds(j, 1), lanes]
                sum_n = sum_n + jnp.sum(n_grad, axis=1, keepdims=True)
                sum_nn = sum_nn + jnp.sum(n_grad * normed, axis=1, keepdims=True)
                n_grads.append(n_grad)
            for part in range(parts):
                lanes = pl.ds(part * TILE, TILE)
                rows_grad = factor * (
                    n_grads[part] - sum_n * (1.0 / D) - normed_of[j, at, lanes] * (sum_nn * (1.0 / D)))
                rows_grad = rows_grad.astype(BF16).astype(F32)
                g = xg[j, 1, quarter(part, b), :].astype(F32)
                moved = g + score_grad * par[pl.ds(2 * J + j, 1), lanes] + rows_grad
                xg[j, 1, quarter(part, b), :] = moved.astype(BF16)

        loop(R // BLOCK, backward)
        send_home(j, 1)

    last = jnp.maximum(z, H - 1 - z)
    grads[...] = jnp.zeros_like(grads)

    def sent(i):
        for d in range(1, G):
            disp_copy(i // 2, i % 2, d, (e + d) % G).wait_send()

    def starts(up):
        return jnp.where(up == 1, z == 0, z == H - 1)

    def passes(up, to):
        return jnp.where(up == 1, (z > 0) & (z < to), (z < H - 1) & (z > to))

    def begin(to, j, up):
        def both(size):
            for a in range(2):
                for piece in range(PIECES):
                    red_copy(a, j, piece, to, up, size).start()

        with_rows(to, both)

    def pass_sum(a, j, to, up):
        def both(size):
            for piece in range(PIECES):
                red_in(a, j, piece, to, size).wait_recv()
                at = (a, j, to, pl.ds(*piece_of(size, piece)))
                sbuf[at] = (sbuf[at].astype(F32) + rbuf[at].astype(F32)).astype(BF16)
                red_copy(a, j, piece, to, up, size).start()

        with_rows(to, both)

    def item(q):
        s, j = q // J, q % J

        def forwarded(i):
            up, a = 1 - i // 2, i % 2
            chunk = jnp.where(up == 1, z - s, z + s)

            @pl.when((s > 0) & (chunk >= 0) & (chunk < H))
            def _():
                def pass_on(size):
                    gat_copy(a, j, chunk, up, size).wait_recv()
                    send_gat(a, j, chunk, up, size)

                with_rows(chunk, pass_on)

        loop(4, forwarded)

        def side(d):
            chunk = jnp.where(d == 0, z - s, z + s)

            @pl.when((chunk >= 0) & (chunk < H) & ((s > 0) | (d == 0)))
            def _():
                compute(chunk, j)

                @pl.when(starts(d) & (s > 0) & ((s > 1) | (j < J - 1)))
                def _():
                    begin(chunk, j, d)

        loop(2, side)

        def through(i):
            a, up = i // 2, (i + jnp.where(z >= H // 2, 0, 1)) % 2
            to = jnp.where(up == 1, s, H - 1 - s)
            near = (to == z + 2 * up - 1) & (j == J - 1) & (s < H - 1)

            @pl.when((s > 0) & passes(up, to) & jnp.logical_not(near))
            def _():
                pass_sum(a, j, to, up)

        loop(4, through)

        @pl.when(q == H * J - 1)
        def _():
            for up in range(2):
                to = z + 2 * up - 1

                @pl.when(starts(up) & (to >= 0) & (to < H))
                def _(up=up, to=to):
                    begin(to, J - 1, up)

                @pl.when(passes(up, to) & (jnp.where(up == 1, to, H - 1 - to) < H - 1))
                def _(up=up, to=to):
                    loop(2, lambda a: pass_sum(a, J - 1, to, up))

        @pl.when((s == last) & (j == 0))
        def _():
            for d in range(1, H):
                zs_copy(d, (z - d + H) % H).wait_recv()
            both = zs[0]
            for h in range(1, H):
                both = both + zs[h]
            mg[e] = both[0:8] / jnp.maximum(both[8:16], 1.0)
            for d in range(1, G):
                mg_copy(d, e).start()

        @pl.when(s == last)
        def _():
            outer(gat[0, j], pg.at[j], o_win.at[j], D, F)
            outer(act[j], gat.at[1, j], o_wout.at[j], F, D)

    loop(H * J, item)
    loop(2 * J, sent)
    loop(J, finish)
    for d in range(1, H):
        gb_copy(d, z, (z + d) % H).start()

    gbuf[z] = grads[:, own_cols]
    for d in range(1, G):
        mg_copy(d, (e - d + G) % G).wait_recv()
    means = jnp.zeros((8, 128), F32)
    for k in range(G):
        v = mg[k] if k == 0 else pltpu.roll(mg[k], k * J, 1)
        means = jnp.where((lane8 >= k * J) & (lane8 < k * J + J), v, means)
    o_mean[...] = means[0:1, 0:E]

    for d in range(1, H):
        gb_copy(d, (z - d + H) % H, z).wait_recv()
    small = gbuf[0]
    for h in range(1, H):
        small = small + gbuf[h]
    o_gain[...] = small[0:J]
    o_bias[...] = small[J:2 * J]
    o_cent[...] = small[2 * J:3 * J]
    o_bout[...] = small[3 * J:4 * J]

    for d in range(1, H):
        par_copy(d, z).wait_send()
        zs_copy(d, z).wait_send()
        gb_copy(d, z, (z + d) % H).wait_send()
    for d in range(1, G):
        mg_copy(d, e).wait_send()

    def drain(i):
        a, j, h = i // (J * H), i // H % J, i % H

        def wait(size):
            @pl.when((z < H - 1) & (h <= z))
            def _():
                gat_copy(a, j, h, 1, size).wait_send()

            @pl.when((z > 0) & (h >= z))
            def _():
                gat_copy(a, j, h, 0, size).wait_send()

            @pl.when(h != z)
            def _():
                for piece in range(PIECES):
                    red_copy(a, j, piece, h, jnp.where(h > z, 1, 0), size).wait_send()

        with_rows(h, wait)

    loop(2 * J * H, drain)

    def arrived(i):
        j, a = i // 2, i % 2
        for d in range(1, G):
            ret_in(j, a, d).wait_recv()
            ret_copy(j, a, d, (e + d) % G).wait_send()

    loop(2 * J, arrived)


def deliver_kernel(dims, home, ret, slot, *refs):
    G, H, J, S, MSG, R, T, D, F, PW, seq_len = dims
    results, (o_mixed, o_tg, *outs), (mixed, moved, sem) = refs[:8], refs[8:18], refs[18:]
    copies = [pltpu.make_async_copy(a, b, sem.at[i]) for i, (a, b) in enumerate(zip(results, outs))]
    for i in (3, 5, 0, 1, 2, 4, 6, 7):
        copies[i].start()

    spot = jnp.transpose(jnp.broadcast_to(slot[pl.ds(0, 1), :].astype(F32), (128, T)))[:, 0:1].astype(jnp.int32)
    live_rows = spot >= 0
    m = iota((T, J * G * MSG), 1)
    for part in range(D // TILE):
        take = ones_where(spot + part * S == m)
        at = pl.ds(part * TILE, TILE)
        for a, to in enumerate((mixed, moved)):
            kept = home[a, pl.ds(part * T, T), :].astype(F32)
            to[:, at] = jnp.where(live_rows, contract(take, ret[a]), kept).astype(BF16)
    for i, (a, b) in enumerate(((mixed, o_mixed), (moved, o_tg))):
        copies.append(pltpu.make_async_copy(a, b, sem.at[8 + i]))
        copies[-1].start()
    for copy in copies:
        copy.wait()


def on_device(
    tokens, assignment, lengths, centroids, ln_gain, ln_bias, w_in, b_in, w_out, b_out, cotangent
):
    T, D = tokens.shape
    G, H = lax.axis_size("expert"), lax.axis_size("hidden")
    J, F = w_in.shape[0], w_in.shape[2]
    PW = centroids.shape[1]
    S = max(2, 9 * T // (8 * J * G))
    parts = D // TILE
    MSG = -(-(parts * S + 1) // 16) * 16
    R, GM, N = G * S, G * MSG, H * G * S
    seq_len = min(2048, H * T)
    dims = (G, H, J, S, MSG, R, T, D, F, PW, seq_len)
    vm = pl.BlockSpec(memory_space=pltpu.VMEM)
    hbm = pl.BlockSpec(memory_space=pl.ANY)
    sm = pl.BlockSpec(memory_space=pltpu.SMEM)
    dma = pltpu.SemaphoreType.DMA
    buffers = [
        ((J, D, F), BF16),
        ((J, F, D), BF16),
        ((2, J, N, D), BF16),
        ((J, N, F), BF16),
        ((J, N, F), BF16),
        ((2, J, H, R, D), BF16),
        ((2, J, H + 1, R, D), BF16),
        ((J, 2, GM, TILE), BF16),
        ((J, 2, GM, TILE), BF16),
        ((J, 2, parts * R, TILE), BF16),
        ((GM, parts * T), BF16),
        ((parts * R, GM), BF16),
        ((GM, parts * R), BF16),
        ((R, GM), BF16),
        ((4 * J, D), F32),
        ((4, J, R, 1), F32),
        ((H, 16, 128), F32),
        ((G, 8, 128), F32),
        ((4 * J, D), F32),
        ((H, 4 * J, PW), F32),
        ((J, R, D), F32),
        ((max(D, F), N), BF16),
    ]
    taken = sum(
        jnp.dtype(t).itemsize * -(-s[-1] // 128) * 128 * functools.reduce(lambda a, b: a * b, s[:-1]) for s, t in buffers
    )

    results = [(J, PW), (J, PW), (J, PW), (J, D, F), (J, F), (J, F, D), (J, PW), (1, G * J)]
    shape = jax.ShapeDtypeStruct

    def layer(number, sizes, *args):
        made = pl.pallas_call(
            functools.partial(layer_kernel, dims, sizes),
            name="layer",
            out_shape=[
                pltpu.VMEM((2, parts * T, TILE), BF16),
                pltpu.VMEM((2, J * GM, TILE), BF16),
                pltpu.VMEM((8, T), jnp.int32),
                *[pltpu.VMEM(s, F32) for s in results],
            ],
            in_specs=[vm, sm, vm, vm, vm, vm, vm, hbm, hbm, hbm, hbm],
            out_specs=[vm] * 11,
            scratch_shapes=[
                *[pltpu.VMEM(s, t) for s, t in buffers],
                dma((2 * parts + 2,)),
                dma((H,)), dma((H,)),
                dma((H,)), dma((H,)),
                dma((G,)), dma((G,)),
                dma((H,)), dma((H,)),
                dma((J, 2, G)), dma((J, 2, G)),
                dma((J, 2, G)), dma((J, 2, G)),
                dma((2, 2, J, H)), dma((2, J, H)),
                dma((2, J, PIECES, H)), dma((2, J, PIECES, H + 1)),
            ],
            compiler_params=pltpu.CompilerParams(
                collective_id=number, has_side_effects=True, vmem_limit_bytes=taken + 3 * 2**20
            ),
            cost_estimate=pl.CostEstimate(
                flops=12 * J * N * D * F, bytes_accessed=30 * 2**20, transcendentals=J * N * F
            ),
        )(*args)
        return pl.pallas_call(
            functools.partial(deliver_kernel, dims),
            name="deliver",
            out_shape=[shape((T, D), BF16), shape((T, D), BF16), *[shape(s, F32) for s in results]],
            in_specs=[vm] * 11,
            out_specs=[hbm] * 10,
            scratch_shapes=[pltpu.VMEM((T, D), BF16), pltpu.VMEM((T, D), BF16), dma((10,))],
            compiler_params=pltpu.CompilerParams(vmem_limit_bytes=8 * 2**20),
        )(*made)

    args = (
        assignment.reshape(1, T), lengths, centroids, ln_gain, ln_bias, b_out, b_in, tokens, cotangent, w_in, w_out
    )
    options = []
    for shares in SHAPES:
        needed = [-(-G * shares[4 * h // H] // 8) * S for h in range(H)]
        options.append(tuple(-(-r // 16) * 16 for r in needed))
    bits = G.bit_length()
    if len(options) > 1 and seq_len == H * T and bits * H < 32:
        alive = lengths[:, None] > jnp.asarray([h * T for h in range(H)], jnp.int32)
        packed = jnp.sum(jnp.where(alive, jnp.asarray([1 << bits * h for h in range(H)], jnp.int32), 0))
        which = jnp.int32(0)
        for i, rows in enumerate(options[1:]):
            fits = True
            for h in range(H):
                fits = fits & ((packed >> (bits * h)) % (1 << bits) * S <= rows[h])
            which = jnp.where(fits, i + 1, which)
    elif len(options) > 1:
        first = (jnp.arange(G, dtype=jnp.int32)[:, None] * H + jnp.arange(H, dtype=jnp.int32)[None, :]) * T
        needed = S * jnp.sum((lengths[first // seq_len] > first % seq_len).astype(jnp.int32), axis=0)
        fits = jnp.all(needed[None, :] <= jnp.asarray(options, jnp.int32), axis=1)
        which = jnp.max(jnp.where(fits, jnp.arange(len(options), dtype=jnp.int32), 0))

    def choose(low, high):
        if high - low == 1:
            return functools.partial(layer, low, options[low])
        middle = (low + high) // 2
        return lambda *args: lax.cond(which >= middle, choose(middle, high), choose(low, middle), *args)

    outs = choose(0, len(options))(*args)
    return (*outs[:9], outs[9].reshape(G * J))


def solution(mesh):
    tok = P(("expert", "hidden"), None)
    par = P("expert", "hidden")
    win = P("expert", None, "hidden")
    wout = P("expert", "hidden", None)
    return jax.shard_map(
        on_device,
        mesh=mesh,
        in_specs=(tok, tok, P(), par, par, par, win, par, wout, par, tok),
        out_specs=(tok, tok, par, par, par, win, par, wout, par, P()),
        check_vma=False,
    )
```

profile of v0, /device:TPU:0, one launch (start us, length us, event | category | flops | bytes accessed | tf_op | source)
XLA Modules:
  0.0 138.8 jit_solution(13517416132295039699)
XLA Ops:
  0.7 1.4 select_reduce_fusion
  4.7 133.9 %conditional.2 = ((bf16[256,1024]{1,0:T(8,128)(2,1)}, bf16[256,1024]{1,0:T(8,128)(2,1)}, f32[2,256]{1,0:T(2,128)}, f32[2,256]{1,0:T(2,128)}, f32[2,256]{1,0:T(2,...) conditional(s32[]{:T(128)} %convert_element_type.6, ...), branch_computations={%region_1.2_spmd, %region_2.5_spmd} | conditional | flops 14495514624 | bytes 31457470 | solution.py:762
  4.7 133.6 %conditional = (bf16[256,1024]{1,0:T(8,128)(2,1)}, bf16[256,1024]{1,0:T(8,128)(2,1)}, f32[2,256]{1,0:T(2,128)}, f32[2,256]{1,0:T(2,128)}, f32[2,256]{1,0:T(2,128...) conditional(s32[]{:T(128)} %convert_element_type.4, ...), branch_computations={%region_3.3_spmd, %region_4.4_spmd} | conditional | flops 14495514624 | bytes 31457360 | solution.py:762
  4.9 126.8 %layer.4 = (bf16[2,1024,256]{2,1,0:T(8,128)(2,1)S(1)}, bf16[2,1280,256]{2,1,0:T(8,128)(2,1)S(1)}, s32[8,256]{1,0:T(8,128)S(1)}, f32[2,256]{1,0:T(2,128)S(1)}, f3...) custom-call(s32[1,256]{1,0:T(1,128)} %get-tuple-element.164.asg, ...), custom_call_target="tpu_custom_call" | custom-call | flops 14495514624 | bytes 31457280 | tf_op jit(solution)/shard_map/cond/branch_1_fun/cond/branch_0_fun/layer/pallas_call | solution.py:695
  131.7 6.4 %deliver.4 = (bf16[256,1024]{1,0:T(8,128)(2,1)}, bf16[256,1024]{1,0:T(8,128)(2,1)}, f32[2,256]{1,0:T(2,128)}, f32[2,256]{1,0:T(2,128)}, f32[2,256]{1,0:T(2,128)}...) custom-call(bf16[2,1024,256]{2,1,0:T(8,128)(2,1)S(1)} %get-tuple-ele, ...), custom_call_target="tpu_custom_call" | custom-call | tf_op jit(solution)/shard_map/cond/branch_1_fun/cond/branch_0_fun/deliver/pallas_call | solution.py:725
  (1 shorter events, 0.0 us)
where the time goes:
time: 139 us
  Pallas kernels  133 us (96%)
  between operations  3.53 us (3%)
    pallas_call x1, Pallas kernels, layer(): pl.pallas_call(functools.partial(layer_kernel, dims, sizes), name='layer'...  127 us
    pallas_call x1, Pallas kernels, layer(): pl.pallas_call(functools.partial(deliver_kernel, dims), name='deliver', o...  6.36 us

commit v1 on v0

--- a/solution.py
+++ b/solution.py
@@ -521,7 +521,7 @@
         def through(i):
             a, up = i // 2, (i + jnp.where(z >= H // 2, 0, 1)) % 2
             to = jnp.where(up == 1, s, H - 1 - s)
-            near = (to == z + 2 * up - 1) & (j == J - 1) & (s < H - 1)
+            near = (a == 1) & (to == z + 2 * up - 1) & (j == J - 1) & (s < H - 1)
 
             @pl.when((s > 0) & passes(up, to) & jnp.logical_not(near))
             def _():
@@ -540,7 +540,7 @@
 
                 @pl.when(passes(up, to) & (jnp.where(up == 1, to, H - 1 - to) < H - 1))
                 def _(up=up, to=to):
-                    loop(2, lambda a: pass_sum(a, J - 1, to, up))
+                    pass_sum(1, J - 1, to, up)
 
         @pl.when((s == last) & (j == 0))
         def _():

time: 139 us -> 129 us (0.928)
  the two profiles are of different devices: /device:TPU:0 before, /device:TPU:11 now
where the time goes in v1:
time: 129 us; the launch traced here: 128 us
  Pallas kernels  123 us (95%)
  between operations  3.53 us (3%)
  other arithmetic  1.39 us (1%)
    pallas_call x1, Pallas kernels, layer(): pl.pallas_call(functools.partial(layer_kernel, dims, sizes), name='layer'...  117 us
    pallas_call x1, Pallas kernels, layer(): pl.pallas_call(functools.partial(deliver_kernel, dims), name='deliver', o...  6.36 us

profile of v1, /device:TPU:11, one launch (start us, length us, event | category | flops | bytes accessed | tf_op | source)
XLA Modules:
  0.0 128.5 jit_solution(6926901133502224093)
XLA Ops:
  0.7 1.4 %select_reduce_fusion = s32[]{:T(128)} fusion(s32[4]{0:T(128)} %constant.66.clone, s32[8]{0:T(128)} %param.19, s32[4]{0:T(128)S(1)} %iota_multiply_fusion), kind=kLoop, calls=%fused_computation | loop fusion | flops 95 | bytes 68 | tf_op jit(solution)/shard_map/reduce_sum | solution.py:745
  4.7 123.5 %conditional.2 = ((bf16[256,1024]{1,0:T(8,128)(2,1)}, bf16[256,1024]{1,0:T(8,128)(2,1)}, f32[2,256]{1,0:T(2,128)}, f32[2,256]{1,0:T(2,128)}, f32[2,256]{1,0:T(2,...) conditional(s32[]{:T(128)} %convert_element_type.6, ...), branch_computations={%region_1.2_spmd, %region_2.5_spmd} | conditional | flops 14495514624 | bytes 31457470 | solution.py:762
  4.7 123.3 %conditional = (bf16[256,1024]{1,0:T(8,128)(2,1)}, bf16[256,1024]{1,0:T(8,128)(2,1)}, f32[2,256]{1,0:T(2,128)}, f32[2,256]{1,0:T(2,128)}, f32[2,256]{1,0:T(2,128...) conditional(s32[]{:T(128)} %convert_element_type.4, ...), branch_computations={%region_3.3_spmd, %region_4.4_spmd} | conditional | flops 14495514624 | bytes 31457360 | solution.py:762
  5.0 116.6 %layer.5 = (bf16[2,1024,256]{2,1,0:T(8,128)(2,1)S(1)}, bf16[2,1280,256]{2,1,0:T(8,128)(2,1)S(1)}, s32[8,256]{1,0:T(8,128)S(1)}, f32[2,256]{1,0:T(2,128)S(1)}, f3...) custom-call(s32[1,256]{1,0:T(1,128)} %get-tuple-element.196.asg, ...), custom_call_target="tpu_custom_call" | custom-call | flops 14495514624 | bytes 31457280 | tf_op jit(solution)/shard_map/cond/branch_1_fun/cond/branch_1_fun/layer/pallas_call | solution.py:695
  121.6 6.4 %deliver.5 = (bf16[256,1024]{1,0:T(8,128)(2,1)}, bf16[256,1024]{1,0:T(8,128)(2,1)}, f32[2,256]{1,0:T(2,128)}, f32[2,256]{1,0:T(2,128)}, f32[2,256]{1,0:T(2,128)}...) custom-call(bf16[2,1024,256]{2,1,0:T(8,128)(2,1)S(1)} %get-tuple-ele, ...), custom_call_target="tpu_custom_call" | custom-call | tf_op jit(solution)/shard_map/cond/branch_1_fun/cond/branch_1_fun/deliver/pallas_call | solution.py:725
  (1 shorter events, 0.0 us)
